TPU v7x, 32 devices: a whole 2x2x4 slice. The times are simulated.
32 devices in a mesh: groups: 2 (over x), expert: 16 (over z, y, core).
Axes of the slice: x: 2, y: 2, z: 4, core: 2. Of those that a mesh axis runs over, the one named last changes fastest.
Arguments:
- queries: bfloat16 [1024, 4096], P(('groups', 'expert')), parts along dimension 0, may hold values from -6 to 6
- incoming_key_value: bfloat16 [1024, 512], P(('groups', 'expert')), parts along dimension 0, may hold values from -6 to 6
- key_value_codes: bfloat16 [4096, 16, 512], P(('groups', 'expert')), parts along dimension 0, may hold values from -6 to 6
- key_value_scales: bfloat16 [4096, 4, 16], P(('groups', 'expert')), parts along dimension 0, may hold values from 0.25 to 96
- lengths: int32 [32, 32], P(('groups', 'expert')), parts along dimension 0, may hold values from 1 to 64, 1024 in all within a row
- block_table: int32 [32, 32, 4], P(('groups', 'expert')), parts along dimension 0, may hold values from 0 to 127, as said below
- hidden: bfloat16 [1024, 2048], P(('groups', 'expert')), parts along dimension 0, may hold values from -6 to 6
- routes: int32 [1024, 8], P(('groups', 'expert')), parts along dimension 0, may hold values from 0 to 15, all different within a row; in each aligned block of 32 rows (0 to 31, 32 to 63, ...) at most 32 rows name the same one
- router: bfloat16 [2048, 16], replicated, may hold values from -0.125 to 0.125
- w_gate: bfloat16 [16, 2048, 768], P('expert'), may hold values from -0.125 to 0.125
- w_up: bfloat16 [16, 2048, 768], P('expert'), may hold values from -0.125 to 0.125
- w_down: bfloat16 [16, 768, 2048], P('expert'), may hold values from -0.21875 to 0.21875
Outputs:
- attn_out: bfloat16 [1024, 4096], P(('groups', 'expert')), parts along dimension 0
- moe_out: bfloat16 [1024, 2048], P(('groups', 'expert')), parts along dimension 0
There are 2 independent parts, one for each index of `groups`. A program takes and returns all parts, laid end to end along the dimension named above; an argument that names none is the same for every part. Nothing has to cross between parts.
Inputs may be any that keep to these rules, and one draw needn't show every extreme that they name: The 32 lengths of one device sum to 1024, and one of them equals 64. `block_table`: on each device the 32 x 4 entries name each of the 128 pool slots exactly once. `routes`: each row names 8 different experts; at most 32 rows of one device name the same expert, and exactly 32 do for some expert and device.
All inputs are finite; a program needn't handle non-finite values.
Results may differ from a plain program's by a relative error of at most 0.0085.
Values may be sent and summed in bfloat16 or wider, within the bound.
A program may use at most 64 MiB of HBM per device.

v0:
```python
import math

import jax
import jax.numpy as jnp
from jax import lax
from jax.sharding import PartitionSpec as P

QUERY_HEADS = 32
KEY_VALUE_HEADS = 2
HEAD_SIZE = 128


def attend(
    query_row_block,
    newest_key_value,
    device_block_codes,
    device_block_scales,
    prompt_lens,
    block_row_slice,
):
    count_of_rows = query_row_block.shape[0]
    block_list = block_row_slice.shape[1]
    block_length = device_block_codes.shape[1]
    context_tokens = block_list * block_length
    head_groups = QUERY_HEADS // KEY_VALUE_HEADS
    inv_root = 1.0 / math.sqrt(HEAD_SIZE)
    cached_entries = device_block_codes[block_row_slice].reshape(
        count_of_rows, context_tokens, 2, KEY_VALUE_HEADS, HEAD_SIZE
    )
    scale_values = device_block_scales[block_row_slice].reshape(
        count_of_rows, block_list, 2, KEY_VALUE_HEADS, block_length
    )
    scale_values = (
        jnp.transpose(scale_values, (0, 2, 3, 1, 4))
        .reshape(count_of_rows, 2, KEY_VALUE_HEADS, context_tokens)
        .astype(jnp.float32)
    )
    query_head_count = query_row_block.reshape(
        count_of_rows, KEY_VALUE_HEADS, head_groups, HEAD_SIZE
    )
    key_codes = cached_entries[:, :, 0]
    value_codes = cached_entries[:, :, 1]
    raw_dots = jnp.einsum(
        "rhgd,rthd->rhgt", query_head_count, key_codes, preferred_element_type=jnp.float32
    )
    scores = raw_dots * scale_values[:, 0][:, :, None, :] * inv_root
    newest_key = newest_key_value[:, : KEY_VALUE_HEADS * HEAD_SIZE].reshape(
        count_of_rows, KEY_VALUE_HEADS, HEAD_SIZE
    )
    newest_value = (
        newest_key_value[:, KEY_VALUE_HEADS * HEAD_SIZE :]
        .reshape(count_of_rows, KEY_VALUE_HEADS, HEAD_SIZE)
        .astype(jnp.float32)
    )
    own_score = (
        jnp.einsum(
            "rhgd,rhd->rhg", query_head_count, newest_key, preferred_element_type=jnp.float32
        )
        * inv_root
    )
    live_mask = (jnp.arange(context_tokens, dtype=jnp.int32)[None, :] < prompt_lens[:, None])[
        :, None, None, :
    ]
    masked = jnp.where(live_mask, scores, -1e30)
    peak_score = jnp.maximum(jnp.max(masked, axis=-1), own_score)
    exp_terms = jnp.where(live_mask, jnp.exp(masked - peak_score[..., None]), 0.0)
    own_exp = jnp.exp(own_score - peak_score)
    totals = jnp.sum(exp_terms, axis=-1) + own_exp
    weights = (exp_terms / totals[..., None] * scale_values[:, 1][:, :, None, :]).astype(
        jnp.bfloat16
    )
    own_weight = (own_exp / totals).astype(jnp.bfloat16)
    mixture = jnp.einsum(
        "rhgt,rthd->rhgd", weights, value_codes, preferred_element_type=jnp.float32
    )
    mixture = mixture + own_weight.astype(jnp.float32)[..., None] * newest_value[:, :, None, :]
    return mixture.reshape(count_of_rows, QUERY_HEADS * HEAD_SIZE).astype(jnp.bfloat16)


def local(
    queries,
    incoming_key_value,
    key_value_codes,
    key_value_scales,
    lengths,
    block_table,
    hidden,
    routes,
    router,
    w_gate,
    w_up,
    w_down,
):
    count_of_rows = hidden.shape[0]
    top_count = routes.shape[1]
    experts = router.shape[1]
    capacity = 2 * count_of_rows * top_count // experts
    flat_routes = routes.reshape(count_of_rows * top_count)
    columns = jnp.arange(experts, dtype=jnp.int32)
    expert_hits = (flat_routes[:, None] == columns[None, :]).astype(jnp.int32)
    slot_rank = jnp.sum((jnp.cumsum(expert_hits, axis=0) - expert_hits) * expert_hits, axis=1)
    slot_index = flat_routes * capacity + slot_rank
    slot_hot = (
        slot_index[:, None] == jnp.arange(experts * capacity, dtype=jnp.int32)[None, :]
    ).reshape(count_of_rows, top_count, experts * capacity)
    logits = jnp.dot(hidden, router, preferred_element_type=jnp.float32)
    chosen = jnp.sum(
        jnp.where(routes[:, :, None] == columns[None, None, :], logits[:, None, :], 0.0), axis=2
    )
    gate_probs = jax.nn.softmax(chosen, axis=-1).astype(jnp.bfloat16)
    device_block_codes, device_block_scales = (
        lax.all_to_all(key_value_codes, "expert", split_axis=0, concat_axis=0, tiled=True),
        lax.all_to_all(key_value_scales, "expert", split_axis=0, concat_axis=0, tiled=True),
    )
    dispatch_matrix = jnp.any(slot_hot, axis=1).astype(jnp.bfloat16)
    outgoing = jnp.einsum(
        "rs,rd->sd", dispatch_matrix, hidden, preferred_element_type=jnp.float32
    ).astype(jnp.bfloat16)
    received = lax.all_to_all(outgoing, "expert", split_axis=0, concat_axis=0, tiled=True)
    gate_part = jnp.dot(received, w_gate[0], preferred_element_type=jnp.float32)
    up_part = jnp.dot(received, w_up[0], preferred_element_type=jnp.float32)
    inner_act = (jax.nn.silu(gate_part) * up_part).astype(jnp.bfloat16)
    results = jnp.dot(inner_act, w_down[0], preferred_element_type=jnp.float32).astype(jnp.bfloat16)
    returned = lax.all_to_all(results, "expert", split_axis=0, concat_axis=0, tiled=True)
    combine_weights = jnp.sum(
        jnp.where(slot_hot, gate_probs.astype(jnp.float32)[:, :, None], 0.0), axis=1
    ).astype(jnp.bfloat16)
    moe_out = jnp.dot(combine_weights, returned, preferred_element_type=jnp.float32).astype(
        jnp.bfloat16
    )
    attn_out = attend(
        queries,
        incoming_key_value,
        device_block_codes,
        device_block_scales,
        lengths[0],
        block_table[0],
    )
    return (attn_out, moe_out)


def solution(mesh):
    in_specs = (
        P(("groups", "expert"), None),
        P(("groups", "expert"), None),
        P(("groups", "expert"), None, None),
        P(("groups", "expert"), None, None),
        P(("groups", "expert"), None),
        P(("groups", "expert"), None, None),
        P(("groups", "expert"), None),
        P(("groups", "expert"), None),
        P(),
        P("expert", None, None),
        P("expert", None, None),
        P("expert", None, None),
    )
    out_specs = (P(("groups", "expert"), None), P(("groups", "expert"), None))
    return jax.shard_map(local, mesh=mesh, in_specs=in_specs, out_specs=out_specs, check_vma=False)
```

profile of v0, /device:TPU:9, one launch (start us, length us, event | category | flops | bytes accessed | tf_op | source)
XLA Modules:
  0.0 174.8 jit_solution(17760913751162859660)
XLA Ops:
  0.6 0.0 copy-start
  0.6 1.0 copy.48
  1.6 0.8 reshape.193
  2.4 6.6 %all-to-all-start.1 = ((bf16[16,2,256]{2,1,0:T(2,128)(2,1)}), bf16[16,2,256]{2,1,0:T(2,128)(2,1)S(1)}, u32[]{:S(2)}, u32[]{:S(2)}) async-start(bf16[16,2,256]{2,1,0:T(2,128)(2,1)} %reshape.193), calls=%async_computation.1 | async-start | bytes 32768 | tf_op jit(solution)/shard_map/all_to_all | solution.py:113
  9.0 0.8 copy.55
  9.8 0.1 eq.56
  9.9 0.1 eq.52
  10.0 0.6 reduce-window.6
  10.6 0.2 slice_reduce_fusion
  10.8 0.1 fusion.27
  10.9 0.1 reduce_sum.49
  11.0 0.0 copy-start.4
  11.0 0.6 copy-done.4
  11.6 0.2 fusion.17
  11.8 3.0 %convolution_convert_fusion = bf16[512,2048]{1,0:T(8,128)(2,1)} fusion(pred[32,512]{1,0:T(8,128)(4,1)S(1)} %fusion.17, bf16[32,2048]{1,0:T(8,128)(2,1)} %param.18), kind=kOutput, calls=%fused_computation.9 | convolution fusion | flops 68157440 | bytes 2244608 | tf_op jit(solution)/shard_map/rs,rd->sd/dot_general | solution.py:116
  14.8 0.0 all-to-all-done.1
  14.8 54.0 %all_to_all.34 = bf16[16,32,2048]{2,1,0:T(8,128)(2,1)} all-to-all(bf16[16,32,2048]{2,1,0:T(8,128)(2,1)} %bitcast.82), channel_id=1, replica_groups=mesh['groups'=2,'expert'=16] {'expert'}, dimensions={0} | all-to-all | bytes 4194304 | tf_op jit(solution)/shard_map/all_to_all | solution.py:119
  68.8 0.0 copy-done.7
  68.8 4.6 %all-to-all-start = ((bf16[128,16,512]{2,1,0:T(8,128)(2,1)}), bf16[128,16,512]{2,1,0:T(8,128)(2,1)}, u32[]{:S(2)}, u32[]{:S(2)}) async-start(bf16[128,16,512]{2,1,0:T(8,128)(2,1)} %param.14), calls=%async_computation | async-start | bytes 4194304 | tf_op jit(solution)/shard_map/all_to_all | solution.py:112
  73.4 5.5 %fusion.4 = f32[512,768]{1,0:T(8,128)} fusion(bf16[512,2048]{1,0:T(8,128)(2,1)} %bitcast.84, bf16[1,2048,768]{2,1,0:T(8,128)(2,1)} %param.21), kind=kOutput, calls=%fused_computation.6 | convolution fusion | flops 1610612736 | bytes 6815744 | tf_op jit(solution)/shard_map/dot_general | solution.py:120
  78.9 0.0 copy-done
  78.9 8.3 %fusion.6 = bf16[512,2048]{1,0:T(8,128)(2,1)} fusion(bf16[1,768,2048]{2,1,0:T(8,128)(2,1)S(1)} %copy-done, f32[512,768]{1,0:T(8,128)} %fusion.4, bf16[512,2048]{1,0:T(8,128)(2,1)} %bitcast.85, bf16[1,2048,768]{2,1,0:T(8,128)(2,1)} %param.22), kind=kOutput, calls=%fused_computation.8 | convolution fusion | flops 3224633344 | bytes 12058624 | tf_op jit(solution)/shard_map/dot_general | solution.py:123
  87.1 32.3 %all-to-all-done = bf16[128,16,512]{2,1,0:T(8,128)(2,1)} async-done(((bf16[128,16,512]{2,1,0:T(8,128)(2,1)}), bf16[128,16,512]{2,1,0:T(8,128)(2,1)}, u32[]{:S(2)}, u32[]{:S(2)}) %all-to-all-start) | async-done | bytes 2097184 | tf_op jit(solution)/shard_map/all_to_all | solution.py:112
  119.5 6.5 %all-to-all-start.3 = ((bf16[16,32,2048]{2,1,0:T(8,128)(2,1)}), bf16[16,32,2048]{2,1,0:T(8,128)(2,1)}, u32[]{:S(2)}, u32[]{:S(2)}) async-start(bf16[16,32,2048]{2,1,0:T(8,128)(2,1)} %bitcast.83), calls=%async_computation.3 | async-start | bytes 4194304 | tf_op jit(solution)/shard_map/all_to_all | solution.py:124
  126.0 0.0 copy-done.9
  126.0 0.6 compare_select_fusion
  126.6 0.8 copy.46
  127.3 0.6 reshape.169
  127.9 0.0 copy-done.2
  127.9 0.7 copy.65
  128.7 0.7 fusion.36
  129.4 0.6 reshape.165
  130.1 0.0 copy-done.1
  130.1 1.0 fusion.39
  131.1 0.7 select_reduce_fusion.1
  131.8 0.1 copy.59
  131.9 0.6 pad_clamp_fusion
  132.5 1.5 select_reduce_fusion
  134.1 0.7 iota_compare_fusion.4
  134.8 1.8 %fusion.38 = f32[32,2,1,16]{3,2,1,0:T(1,128)} fusion(bf16[32,2,16,128]{3,2,1,0:T(8,128)(2,1)} %bitcast.89, bf16[32,2,128,1]{2,3,1,0:T(2,128)(2,1)S(1)} %reshape.191), kind=kOutput, calls=%fused_computation.65 | convolution fusion | flops 262144 | bytes 282624 | tf_op jit(solution)/shard_map/rhgd,rhd->rhg/dot_general | solution.py:56
  136.6 0.9 reshape.194
  137.5 0.7 gather_fusion.1
  138.3 0.1 copy.49
  138.3 0.1 copy.50
  138.5 0.1 copy.51
  138.6 0.1 copy.52
  138.7 0.1 copy.53
  138.8 3.6 %gather_fusion = bf16[128,16,512]{2,1,0:T(8,128)(2,1)} fusion(bf16[128,16,512]{2,1,0:T(8,128)(2,1)} %all-to-all-done, s32[1024]{0:T(1024)S(1)} %pad_clamp_fusion), kind=kCustom, calls=%fused_computation | custom fusion | bytes 4194816 | tf_op jit(solution)/shard_map/gather | solution.py:27
  142.4 4.0 %reshape.160 = bf16[32,64,2,2,128]{4,3,2,1,0:T(2,128)(2,1)} reshape(bf16[128,16,512]{2,1,0:T(8,128)(2,1)} %gather_fusion) | data formatting | bytes 4194304 | tf_op jit(solution)/shard_map/reshape | solution.py:27
  146.4 3.0 %fusion.35 = (bf16[32,64,1,2,128]{4,3,2,1,0:T(2,128)(2,1)S(1)}, bf16[32,64,1,2,128]{4,3,2,1,0:T(2,128)(2,1)S(1)}) fusion(bf16[32,64,2,2,128]{4,3,2,1,0:T(2,128)(2,1)} %reshape.160), kind=kLoop, calls=%fused_computation.62 | loop fusion | bytes 4194304 | tf_op jit(solution)/shard_map/slice | solution.py:41
  149.4 0.0 copy-start.6
  149.4 0.0 copy-start.8
  149.4 0.0 copy-done.3
  149.4 0.8 fusion.37
  150.2 0.0 copy-done.6
  150.2 0.4 fusion.18
  150.6 0.1 fusion.34
  150.7 0.0 copy-done.8
  150.7 0.0 copy-start.5
  150.7 0.5 fusion.14
  151.2 0.8 copy.75
  152.0 20.0 %all-to-all-done.3 = bf16[16,32,2048]{2,1,0:T(8,128)(2,1)} async-done(((bf16[16,32,2048]{2,1,0:T(8,128)(2,1)}), bf16[16,32,2048]{2,1,0:T(8,128)(2,1)}, u32[]{:S(2)}, u32[]{:S(2)}) %all-to-all-start.3) | async-done | bytes 2097184 | tf_op jit(solution)/shard_map/all_to_all | solution.py:124
  172.1 0.0 copy-done.5
  172.1 2.7 %convolution_convert_fusion.1 = bf16[32,2048]{1,0:T(8,128)(2,1)} fusion(bf16[512,2048]{1,0:T(8,128)(2,1)} %bitcast.19, bf16[32,512]{1,0:T(8,128)(2,1)S(1)} %copy-done.5), kind=kOutput, calls=%fused_computation.10 | convolution fusion | flops 67174400 | bytes 2260992 | tf_op jit(solution)/shard_map/dot_general | solution.py:128
  (15 shorter events, 0.2 us)
Async XLA Ops:
  0.6 78.2 %copy-start = (bf16[1,768,2048]{2,1,0:T(8,128)(2,1)S(1)}, bf16[1,768,2048]{2,1,0:T(8,128)(2,1)}, u32[]{:S(2)}) copy-start(bf16[1,768,2048]{2,1,0:T(8,128)(2,1)} %param.23) | copy-start | bytes 9437188
  2.4 12.4 %all-to-all-start.1 = ((bf16[16,2,256]{2,1,0:T(2,128)(2,1)}), bf16[16,2,256]{2,1,0:T(2,128)(2,1)S(1)}, u32[]{:S(2)}, u32[]{:S(2)}) async-start(bf16[16,2,256]{2,1,0:T(2,128)(2,1)} %reshape.193), calls=%async_computation.1 | async-start | bytes 32768 | tf_op jit(solution)/shard_map/all_to_all | solution.py:113
  11.0 0.6 copy-start.4
  14.8 54.0 %copy-start.7 = (bf16[16,2,256]{2,1,0:T(2,128)(2,1)}, bf16[16,2,256]{2,1,0:T(2,128)(2,1)S(1)}, u32[]{:S(2)}) copy-start(bf16[16,2,256]{2,1,0:T(2,128)(2,1)S(1)} %all-to-all-done.1) | copy-start | bytes 49156
  68.8 50.7 %all-to-all-start = ((bf16[128,16,512]{2,1,0:T(8,128)(2,1)}), bf16[128,16,512]{2,1,0:T(8,128)(2,1)}, u32[]{:S(2)}, u32[]{:S(2)}) async-start(bf16[128,16,512]{2,1,0:T(8,128)(2,1)} %param.14), calls=%async_computation | async-start | bytes 4194304 | tf_op jit(solution)/shard_map/all_to_all | solution.py:112
  119.5 6.5 %copy-start.9 = (s32[1,32,4]{1,2,0:T(4,128)S(1)}, s32[1,32,4]{1,2,0:T(4,128)}, u32[]{:S(2)}) copy-start(s32[1,32,4]{1,2,0:T(4,128)} %param.17) | copy-start | bytes 1540
  119.5 8.5 %copy-start.2 = (bf16[32,4096]{1,0:T(8,128)(2,1)S(1)}, bf16[32,4096]{1,0:T(8,128)(2,1)}, u32[]{:S(2)}) copy-start(bf16[32,4096]{1,0:T(8,128)(2,1)} %param.12) | copy-start | bytes 786436
  119.5 10.6 %copy-start.1 = (bf16[32,2048]{1,0:T(8,128)(2,1)S(1)}, bf16[32,2048]{1,0:T(8,128)(2,1)}, u32[]{:S(2)}) copy-start(bf16[32,2048]{1,0:T(8,128)(2,1)} %param.18) | copy-start | bytes 393220
  119.5 52.6 %all-to-all-start.3 = ((bf16[16,32,2048]{2,1,0:T(8,128)(2,1)}), bf16[16,32,2048]{2,1,0:T(8,128)(2,1)}, u32[]{:S(2)}, u32[]{:S(2)}) async-start(bf16[16,32,2048]{2,1,0:T(8,128)(2,1)} %bitcast.83), calls=%async_computation.3 | async-start | bytes 4194304 | tf_op jit(solution)/shard_map/all_to_all | solution.py:124
  146.4 3.0 %copy-start.3 = (bf16[4,8,32,128]{3,2,1,0:T(8,128)(2,1)S(1)}, bf16[4,8,32,128]{3,2,1,0:T(8,128)(2,1)}, u32[]{:S(2)}) copy-start(bf16[4,8,32,128]{3,2,1,0:T(8,128)(2,1)} %copy.65) | copy-start | bytes 786436
  149.4 0.8 copy-start.6
  149.4 1.3 copy-start.8
  150.7 21.3 %copy-start.5 = (bf16[32,512]{1,0:T(8,128)(2,1)S(1)}, bf16[32,512]{1,0:T(8,128)(2,1)}, u32[]{:S(2)}) copy-start(bf16[32,512]{1,0:T(8,128)(2,1)} %select_reduce_fusion) | copy-start | bytes 98308
where the time goes:
time: 177 us; the launch traced here: 175 us
  blocking collectives  54 us (31%)
  waiting for transfers between devices  52.4 us (30%)
  matrix products  23.5 us (13%)
  local copies, waits for them, and re-layouts  19.9 us (11%)
  starting transfers between devices  17.7 us (10%)
  other arithmetic  6.48 us (4%)
    all_to_all x1, blocking collectives, local(): lax.all_to_all(outgoing, 'expert', split_axis=0, concat_axis=0, tiled=True)  54 us
    all_to_all x1, waiting for transfers between devices, local(): lax.all_to_all(key_value_codes, 'expert', split_axis=0, concat_axis=0, ti...  32.3 us
    all_to_all x1, waiting for transfers between devices, local(): lax.all_to_all(results, 'expert', split_axis=0, concat_axis=0, tiled=True)  20 us
    dot_general x1, matrix products, local(): jnp.dot(inner_act, w_down[0], preferred_element_type=jnp.float32)  8.28 us
    all_to_all x1, starting transfers between devices, local(): lax.all_to_all(key_value_scales, 'expert', split_axis=0, concat_axis=0, t...  6.61 us
    all_to_all x1, starting transfers between devices, local(): lax.all_to_all(results, 'expert', split_axis=0, concat_axis=0, tiled=True)  6.48 us
    unnamed x26, local copies, waits for them, and re-layouts  5.58 us
    dot_general x1, matrix products, local(): gate_part = jnp.dot(received, w_gate[0], preferred_element_type=jnp.float32)  5.46 us
  transfers between devices with their start and end apart: 3, of which 2 were waited for; matrix products, arithmetic and copies ran while one was open for 26% of the time, Pallas kernels for 0%

commit v1 on v0

--- a/solution.py
+++ b/solution.py
@@ -1,8 +1,11 @@
+import functools
 import math
 
 import jax
 import jax.numpy as jnp
 from jax import lax
+from jax.experimental import pallas as pl
+from jax.experimental.pallas import tpu as pltpu
 from jax.sharding import PartitionSpec as P
 
 QUERY_HEADS = 32
@@ -139,6 +142,415 @@
     return (attn_out, moe_out)
 
 
+MESH = pl.DeviceIdType.MESH
+F32 = jnp.float32
+BF16 = jnp.bfloat16
+
+
+def fused_kernel(
+    n,
+    q_ref,
+    new_ref,
+    kv_ref,
+    scale_ref,
+    meta_ref,
+    hid_ref,
+    routes_ref,
+    router_ref,
+    wg_hbm,
+    wu_hbm,
+    wd_hbm,
+    attn_ref,
+    moe_ref,
+    x,
+    pool,
+    scales,
+    wg,
+    wu,
+    wd,
+    act,
+    part,
+    r1,
+    r2,
+    r3,
+    qh,
+    m_ref,
+    l_ref,
+    acc,
+    w_sem,
+    own_sem,
+    ag_s,
+    ag_r,
+    kv_s,
+    kv_r,
+    sc_s,
+    sc_r,
+    rs_s,
+    rs_r,
+):
+    rows, width = hid_ref.shape
+    ff = wg.shape[1]
+    experts = router_ref.shape[1]
+    depth = n // 4
+    chips = n // 2
+    heads = KEY_VALUE_HEADS
+    group = QUERY_HEADS // heads
+    tokens = pool.shape[1]
+    me = lax.axis_index("expert")
+    z, y, c = me // 4, (me // 2) % 2, me % 2
+    chip = me // 2
+    sibling = chip * 2 + (1 - c)
+
+    def at(zz, yy, cc):
+        return zz * 4 + yy * 2 + cc
+
+    weights = [
+        pltpu.make_async_copy(s, d, w_sem.at[i])
+        for i, (s, d) in enumerate(((wg_hbm, wg), (wu_hbm, wu), (wd_hbm, wd)))
+    ]
+    for w in weights:
+        w.start()
+    own_kv = pltpu.make_async_copy(kv_ref.at[me], pool.at[me], own_sem.at[0])
+    own_kv.start()
+
+    barrier = pltpu.get_barrier_semaphore()
+    for k in range(1, n):
+        pl.semaphore_signal(
+            barrier, inc=1, device_id={"expert": (me + k) % n}, device_id_type=MESH
+        )
+
+    logits = jnp.dot(hid_ref[...], router_ref[...], preferred_element_type=F32)
+    lane = lax.broadcasted_iota(jnp.int32, (rows, experts), 1)
+    chosen = lane < 0
+    for k in range(routes_ref.shape[1]):
+        chosen = jnp.logical_or(chosen, routes_ref[:, k : k + 1] == lane)
+    logits = jnp.where(chosen, logits, -1e30)
+    terms = jnp.where(chosen, jnp.exp(logits - jnp.max(logits, axis=1, keepdims=True)), 0.0)
+    gates = (terms / jnp.sum(terms, axis=1, keepdims=True)).astype(BF16)
+    spread = (
+        lax.broadcasted_iota(jnp.int32, (experts, 128), 0)
+        == lax.broadcasted_iota(jnp.int32, (experts, 128), 1)
+    ).astype(BF16)
+    x[me, :, :width] = hid_ref[...]
+    x[me, :, width:] = jnp.dot(gates, spread, preferred_element_type=F32).astype(BF16)
+    scales[me] = scale_ref[me]
+
+    pl.semaphore_wait(barrier, n - 1)
+
+    def ag(src, slot, target):
+        return pltpu.make_async_remote_copy(
+            src_ref=x.at[src],
+            dst_ref=x.at[src],
+            send_sem=ag_s.at[slot],
+            recv_sem=ag_r.at[src],
+            device_id={"expert": target},
+            device_id_type=MESH,
+        )
+
+    def kv(dest, source):
+        return pltpu.make_async_remote_copy(
+            src_ref=kv_ref.at[dest],
+            dst_ref=pool.at[source],
+            send_sem=kv_s.at[dest],
+            recv_sem=kv_r.at[source],
+            device_id={"expert": dest},
+            device_id_type=MESH,
+        )
+
+    def sc(dest, source):
+        return pltpu.make_async_remote_copy(
+            src_ref=scale_ref.at[dest],
+            dst_ref=scales.at[source],
+            send_sem=sc_s.at[dest],
+            recv_sem=sc_r.at[source],
+            device_id={"expert": dest},
+            device_id_type=MESH,
+        )
+
+    for d in range(1, depth):
+        ag(me, d - 1, at((z + d) % depth, y, c)).start()
+    ag(me, depth - 1, at(z, 1 - y, c)).start()
+    ag(me, 2 * depth - 1, sibling).start()
+
+    kv_order = [sibling]
+    for j in range(1, chips):
+        for cc in range(2):
+            kv_order.append(((chip + j) % chips) * 2 + (c + cc) % 2)
+    for dest in kv_order:
+        sc(dest, me).start()
+        kv(dest, me).start()
+
+    req_of_row = lax.broadcasted_iota(jnp.int32, (group * rows, 1), 0) % rows
+    for h in range(heads):
+        for g in range(group):
+            at_lane = (h * group + g) * HEAD_SIZE
+            qh[h, g * rows : (g + 1) * rows, :] = q_ref[:, at_lane : at_lane + HEAD_SIZE]
+        k_new = new_ref[:, h * HEAD_SIZE : (h + 1) * HEAD_SIZE].astype(F32)
+        v_new = new_ref[:, (heads + h) * HEAD_SIZE : (heads + h + 1) * HEAD_SIZE].astype(F32)
+        for g in range(group):
+            own = jnp.sum(
+                qh[h, g * rows : (g + 1) * rows, :].astype(F32) * k_new, axis=1, keepdims=True
+            ) * (1.0 / math.sqrt(HEAD_SIZE))
+            m_ref[h, g * rows : (g + 1) * rows, :] = jnp.broadcast_to(own, (rows, HEAD_SIZE))
+            acc[h, g * rows : (g + 1) * rows, :] = v_new
+        first = lax.broadcasted_iota(jnp.int32, (group * rows, HEAD_SIZE), 1) == 0
+        l_ref[h] = jnp.where(first, 1.0, 0.0)
+
+    for d in range(1, depth):
+        src = at((z + depth - d) % depth, y, c)
+        ag(src, 0, sibling).wait_recv()
+        ag(src, depth - 1 + d, at(z, 1 - y, c)).start()
+        ag(src, 2 * depth - 1 + d, sibling).start()
+    for d in range(depth):
+        src = at((z + depth - d) % depth, 1 - y, c)
+        ag(src, 0, sibling).wait_recv()
+        ag(src, 3 * depth - 1 + d, sibling).start()
+    for zz in range(depth):
+        for yy in range(2):
+            ag(at(zz, yy, 1 - c), 0, sibling).wait_recv()
+
+    weights[0].wait()
+    weights[1].wait()
+    tile = 256
+
+    def up_body(t, _):
+        cols = pl.ds(pl.multiple_of(t * tile, tile), tile)
+        xs = x[:, :, :width].reshape(n * rows, width)
+        g = jnp.dot(xs, wg[:, cols], preferred_element_type=F32)
+        u = jnp.dot(xs, wu[:, cols], preferred_element_type=F32)
+        act[:, cols] = (g / (1.0 + jnp.exp(-g)) * u).astype(BF16)
+        return 0
+
+    lax.fori_loop(0, ff // tile, up_body, 0)
+    weights[2].wait()
+    all_gates = x[:, :, width:].reshape(n * rows, 128).astype(F32)
+    here = lax.broadcasted_iota(jnp.int32, (n * rows, 128), 1) == me
+    gate = jnp.sum(jnp.where(here, all_gates, 0.0), axis=1, keepdims=True)
+
+    def down_body(t, _):
+        cols = pl.ds(pl.multiple_of(t * tile, tile), tile)
+        o = jnp.dot(act[...], wd[:, cols], preferred_element_type=F32) * gate
+        part[:, :, cols] = o.astype(BF16).reshape(n, rows, tile)
+        return 0
+
+    lax.fori_loop(0, width // tile, down_body, 0)
+
+    def rs(src, dst, slot, target):
+        return pltpu.make_async_remote_copy(
+            src_ref=src,
+            dst_ref=dst,
+            send_sem=rs_s.at[slot],
+            recv_sem=rs_r.at[slot],
+            device_id={"expert": target},
+            device_id_type=MESH,
+        )
+
+    def to_sibling(zz, yy):
+        slot = zz * 2 + yy
+        return rs(part.at[at(zz, yy, 1 - c)], r1.at[slot], slot, sibling)
+
+    def to_y(zz):
+        return rs(part.at[at(zz, 1 - y, c)], r2.at[zz], 2 * depth + zz, at(z, 1 - y, c))
+
+    def to_z(d):
+        there = at((z + d) % depth, y, c)
+        return rs(part.at[there], r3.at[d - 1], 3 * depth + d - 1, there)
+
+    def attend_chip(j):
+        src_chip = (chip + chips - j) % chips
+        if j == 0:
+            own_kv.wait()
+            kv(sibling, sibling).wait_recv()
+            sc(sibling, sibling).wait_recv()
+        else:
+            for cc in range(2):
+                src = src_chip * 2 + cc
+                kv(sibling, src).wait_recv()
+                sc(sibling, src).wait_recv()
+        span = 2 * tokens
+        peer_blocks = tokens // 16
+        lanes = lax.broadcasted_iota(jnp.int32, (meta_ref.shape[0], span), 1)
+        entry = lax.broadcasted_iota(jnp.int32, (meta_ref.shape[0], span), 0)
+        slot = src_chip * 2 * peer_blocks + lanes // 16
+        live = jnp.logical_and(
+            meta_ref[:, 0:1] == slot, (entry % 4) * 16 + lanes % 16 < meta_ref[:, 1:2]
+        )
+        owner = jnp.sum(jnp.where(live, entry // 4 + 1, 0), axis=0, keepdims=True) - 1
+        pair = pl.ds(src_chip * 2, 2)
+
+        for h in range(heads):
+            keys = pool[pair, :, h * HEAD_SIZE : (h + 1) * HEAD_SIZE].reshape(span, HEAD_SIZE)
+            vals = pool[pair, :, (heads + h) * HEAD_SIZE : (heads + h + 1) * HEAD_SIZE].reshape(
+                span, HEAD_SIZE
+            )
+            k_scale = jnp.concatenate(
+                [scales[src_chip * 2, h : h + 1, :], scales[src_chip * 2 + 1, h : h + 1, :]], axis=1
+            ) * (1.0 / math.sqrt(HEAD_SIZE))
+            v_scale = jnp.concatenate(
+                [
+                    scales[src_chip * 2, heads + h : heads + h + 1, :],
+                    scales[src_chip * 2 + 1, heads + h : heads + h + 1, :],
+                ],
+                axis=1,
+            )
+            step = 128
+
+            def body(t, _):
+                rr = pl.ds(pl.multiple_of(t * step, step), step)
+                s = lax.dot_general(
+                    qh[h, rr, :], keys, (((1,), (1,)), ((), ())), preferred_element_type=F32
+                )
+                req = lax.broadcasted_iota(jnp.int32, (step, span), 0) % rows
+                s = jnp.where(req == owner, s * k_scale, -1e30)
+                m_old = m_ref[h, rr, :]
+                m_new = jnp.maximum(m_old, jnp.max(s, axis=1, keepdims=True))
+                p = jnp.exp(s - jnp.concatenate([m_new, m_new], axis=1))
+                alpha = jnp.exp(m_old - m_new)
+                m_ref[h, rr, :] = m_new
+                l_ref[h, rr, :] = alpha * l_ref[h, rr, :] + p[:, :tokens] + p[:, tokens:]
+                mix = jnp.dot((p * v_scale).astype(BF16), vals, preferred_element_type=F32)
+                acc[h, rr, :] = alpha * acc[h, rr, :] + mix
+                return 0
+
+            lax.fori_loop(0, group * rows // step, body, 0)
+
+    for zz in range(depth):
+        to_sibling(zz, 1 - y).start()
+    for zz in range(depth):
+        to_sibling(zz, y).start()
+    attend_chip(0)
+    for zz in range(depth):
+        to_sibling(zz, 1 - y).wait_recv()
+        there = at(zz, 1 - y, c)
+        part[there] = (part[there].astype(F32) + r1[zz * 2 + 1 - y].astype(F32)).astype(BF16)
+        to_y(zz).start()
+    for zz in range(depth):
+        to_sibling(zz, y).wait_recv()
+        there = at(zz, y, c)
+        part[there] = (part[there].astype(F32) + r1[zz * 2 + y].astype(F32)).astype(BF16)
+    attend_chip(1)
+    for d in range(1, depth):
+        zz = (z + d) % depth
+        to_y(zz).wait_recv()
+        there = at(zz, y, c)
+        part[there] = (part[there].astype(F32) + r2[zz].astype(F32)).astype(BF16)
+        to_z(d).start()
+    to_y(z).wait_recv()
+    for j in range(2, chips):
+        attend_chip(j)
+    total = part[me].astype(F32) + r2[z].astype(F32)
+    for d in range(1, depth):
+        to_z(d).wait_recv()
+        total = total + r3[d - 1].astype(F32)
+    moe_ref[...] = total.astype(BF16)
+
+    for h in range(heads):
+        for g in range(group):
+            rr = slice(g * rows, (g + 1) * rows)
+            at_lane = (h * group + g) * HEAD_SIZE
+            norm = jnp.sum(l_ref[h, rr, :], axis=1, keepdims=True)
+            attn_ref[:, at_lane : at_lane + HEAD_SIZE] = (acc[h, rr, :] / norm).astype(BF16)
+
+    for i in range(n - 1):
+        ag(me, i, sibling).wait_send()
+    for dest in kv_order:
+        sc(dest, me).wait_send()
+        kv(dest, me).wait_send()
+    for zz in range(depth):
+        for yy in range(2):
+            to_sibling(zz, yy).wait_send()
+        to_y(zz).wait_send()
+    for d in range(1, depth):
+        to_z(d).wait_send()
+
+
+def fused_local(
+    n,
+    queries,
+    incoming_key_value,
+    key_value_codes,
+    key_value_scales,
+    lengths,
+    block_table,
+    hidden,
+    routes,
+    router,
+    w_gate,
+    w_up,
+    w_down,
+):
+    rows, width = hidden.shape
+    ff = w_gate.shape[2]
+    blocks, block_tokens, features = key_value_codes.shape
+    tokens = blocks // n * block_tokens
+    depth = n // 4
+    codes = key_value_codes.reshape(n, tokens, features)
+    kinds = key_value_scales.shape[1]
+    scales = jnp.transpose(
+        key_value_scales.reshape(n, blocks // n, kinds, block_tokens), (0, 2, 1, 3)
+    ).reshape(n, kinds, tokens)
+    scales = jnp.pad(scales.astype(jnp.float32), ((0, 0), (0, 8 - kinds), (0, 0)))
+    table = block_table[0]
+    meta = jnp.stack(
+        [table.reshape(-1), jnp.broadcast_to(lengths[0][:, None], table.shape).reshape(-1)], axis=1
+    )
+    q_rows = rows * QUERY_HEADS // KEY_VALUE_HEADS
+    vmem = pl.BlockSpec(memory_space=pltpu.VMEM)
+    hbm = pl.BlockSpec(memory_space=pl.ANY)
+    dma = pltpu.SemaphoreType.DMA
+    return pl.pallas_call(
+        functools.partial(fused_kernel, n),
+        out_shape=(
+            jax.ShapeDtypeStruct(queries.shape, BF16),
+            jax.ShapeDtypeStruct(hidden.shape, BF16),
+        ),
+        in_specs=[vmem, vmem, hbm, vmem, vmem, vmem, vmem, vmem, hbm, hbm, hbm],
+        out_specs=(vmem, vmem),
+        scratch_shapes=[
+            pltpu.VMEM((n, rows, width + 128), BF16),
+            pltpu.VMEM((n, tokens, features), BF16),
+            pltpu.VMEM((n, 8, tokens), F32),
+            pltpu.VMEM((width, ff), BF16),
+            pltpu.VMEM((width, ff), BF16),
+            pltpu.VMEM((ff, width), BF16),
+            pltpu.VMEM((n * rows, ff), BF16),
+            pltpu.VMEM((n, rows, width), BF16),
+            pltpu.VMEM((2 * depth, rows, width), BF16),
+            pltpu.VMEM((depth, rows, width), BF16),
+            pltpu.VMEM((depth - 1, rows, width), BF16),
+            pltpu.VMEM((KEY_VALUE_HEADS, q_rows, HEAD_SIZE), BF16),
+            pltpu.VMEM((KEY_VALUE_HEADS, q_rows, HEAD_SIZE), F32),
+            pltpu.VMEM((KEY_VALUE_HEADS, q_rows, HEAD_SIZE), F32),
+            pltpu.VMEM((KEY_VALUE_HEADS, q_rows, HEAD_SIZE), F32),
+            dma((3,)),
+            dma((1,)),
+            dma((n - 1,)),
+            dma((n,)),
+            dma((n,)),
+            dma((n,)),
+            dma((n,)),
+            dma((n,)),
+            dma((n - 1,)),
+            dma((n - 1,)),
+        ],
+        compiler_params=pltpu.CompilerParams(
+            collective_id=0, has_side_effects=True, vmem_limit_bytes=48 * 1024 * 1024
+        ),
+    )(
+        queries,
+        incoming_key_value,
+        codes,
+        scales,
+        meta,
+        hidden,
+        routes,
+        router,
+        w_gate[0],
+        w_up[0],
+        w_down[0],
+    )
+
+
 def solution(mesh):
     in_specs = (
         P(("groups", "expert"), None),
@@ -155,4 +567,6 @@
         P("expert", None, None),
     )
     out_specs = (P(("groups", "expert"), None), P(("groups", "expert"), None))
-    return jax.shard_map(local, mesh=mesh, in_specs=in_specs, out_specs=out_specs, check_vma=False)
+    n = mesh.shape["expert"]
+    body = functools.partial(fused_local, n) if n == 16 else local
+    return jax.shard_map(body, mesh=mesh, in_specs=in_specs, out_specs=out_specs, check_vma=False)

time: 177 us -> 107 us (0.60); the launches traced: 175 us -> 107 us
  Pallas kernels: 0 us -> 96 us
  blocking collectives: 54 us -> 0 us
  waiting for transfers between devices: 52.4 us -> 0 us
  matrix products: 23.5 us -> 0 us
  starting transfers between devices: 17.7 us -> 0 us
  local copies, waits for them, and re-layouts: 19.9 us -> 10.2 us
  other arithmetic: 6.48 us -> 0.02 us
    pallas_call x0 -> x1, Pallas kernels: none -> 96 us  [fused_local(): pl.pallas_call(functools.partial(fused_kernel, n), out_shape=(jax.ShapeDt...]
    all_to_all x1 -> x0, blocking collectives: 54 us -> none  [local(): lax.all_to_all(outgoing, 'expert', split_axis=0, concat_axis=0, tiled=True)]
    all_to_all x3 -> x0, waiting for transfers between devices: 52.4 us -> none  [the longest x1 32.3 us: local(): lax.all_to_all(key_value_codes, 'expert', split_axis=0, concat_axis=0, ti...]
    dot_general x8 -> x0, matrix products: 23.5 us -> none  [the longest x1 8.28 us: local(): jnp.dot(inner_act, w_down[0], preferred_element_type=jnp.float32)]
    all_to_all x3 -> x0, starting transfers between devices: 17.7 us -> none  [the longest x1 6.61 us: local(): lax.all_to_all(key_value_scales, 'expert', split_axis=0, concat_axis=0, t...]
    gather x3 -> x0, local copies, waits for them, and re-layouts: 4.46 us -> none  [the longest x1 3.62 us: attend(): device_block_codes[block_row_slice]]
    reshape x2 -> x0, local copies, waits for them, and re-layouts: 3.99 us -> none  [the longest x1 3.97 us: attend(): device_block_codes[block_row_slice]]
    unnamed x26 -> x14, local copies, waits for them, and re-layouts: 5.58 us -> 9.04 us
  transfers between devices with their start and end apart: 3 -> 0, of which waited for: 2 -> 0; matrix products, arithmetic and copies ran while one was open for 26% -> 0% of each run, Pallas kernels for 0% -> 0%
where the time goes in v1:
time: 107 us
  Pallas kernels  96 us (90%)
  local copies, waits for them, and re-layouts  10.2 us (10%)
    pallas_call x1, Pallas kernels, fused_local(): pl.pallas_call(functools.partial(fused_kernel, n), out_shape=(jax.ShapeDt...  96 us
    unnamed x14, local copies, waits for them, and re-layouts  9.04 us

profile of v1, /device:TPU:9, one launch (start us, length us, event | category | flops | bytes accessed | tf_op | source)
XLA Modules:
  0.0 107.0 jit_solution(15257744064941398649)
XLA Ops:
  0.6 0.7 broadcast_in_dim.8
  1.4 0.1 stack_reshape.3
  1.5 0.8 copy.29
  2.2 0.1 stack_reshape_squeeze.3
  2.3 0.8 copy.31.routes_ref
  3.1 0.1 copy.30.meta_ref
  3.2 0.8 copy.27
  4.1 0.1 reshape.15
  4.2 1.1 %copy.32.router_ref = bf16[2048,16]{1,0:T(8,128)(2,1)S(1)} copy(bf16[2048,16]{0,1:T(8,128)(2,1)} %param.20) | data formatting | bytes 131072 | tf_op args[8]
  5.4 0.0 copy-start
  5.4 1.6 %copy-done = bf16[128,16,512]{2,1,0:T(8,128)(2,1)S(1)} copy-done((bf16[128,16,512]{2,1,0:T(8,128)(2,1)S(1)}, bf16[128,16,512]{2,1,0:T(8,128)(2,1)}, u32[]{:S(2)}) %copy-start) | copy-done | bytes 2097176
  7.0 0.0 copy-start.1
  7.0 0.9 copy-done.1
  7.9 0.0 copy-start.2
  7.9 0.9 copy-done.2
  8.8 0.0 copy-start.3
  8.8 0.8 copy-done.3
  9.6 96.0 %shard_map.131 = (bf16[32,4096]{1,0:T(8,128)(2,1)S(1)}, bf16[32,2048]{1,0:T(8,128)(2,1)S(1)}) custom-call(bf16[32,4096]{1,0:T(8,128)(2,1)S(1)} %copy-done.1, bf16[32,512]{1,0:T(8,128)(2,1)S(1)} %copy-done.3, bf16[16,128,512]{2,1,0:T(8,128)(2,1)S(1)} %bitcast.12, f32[16,8,128]{2,1,0:T(8,128)S(1)} %pad_convert_fusion.scale_ref, s32[128,2]{1,0:T(8,128)S(1)} %copy.30.meta_ref, ...), custom_call_target="tpu_custom_call" | custom-call | tf_op jit(solution)/shard_map/pallas_call | solution.py:501
  105.6 0.7 copy.36
  106.3 0.7 copy.37
  (3 shorter events, 0.0 us)
Async XLA Ops:
  5.4 1.6 %copy-start = (bf16[128,16,512]{2,1,0:T(8,128)(2,1)S(1)}, bf16[128,16,512]{2,1,0:T(8,128)(2,1)}, u32[]{:S(2)}) copy-start(bf16[128,16,512]{2,1,0:T(8,128)(2,1)} %param.14) | copy-start | bytes 6291460
  7.0 0.9 copy-start.1
  7.9 0.9 copy-start.2
  8.8 0.8 copy-start.3

commit v2 on v1

--- a/solution.py
+++ b/solution.py
@@ -144,24 +144,35 @@
 
 MESH = pl.DeviceIdType.MESH
 F32 = jnp.float32
+LOG2_SCALE = math.log2(math.e) / math.sqrt(HEAD_SIZE)
 BF16 = jnp.bfloat16
 
 
 def fused_kernel(
     n,
-    q_ref,
-    new_ref,
+    q_hbm,
+    new_hbm,
     kv_ref,
-    scale_ref,
-    meta_ref,
-    hid_ref,
-    routes_ref,
-    router_ref,
+    raw_scale_hbm,
+    table_hbm,
+    lengths_hbm,
+    hid_hbm,
+    routes_hbm,
+    router_hbm,
     wg_hbm,
     wu_hbm,
     wd_hbm,
     attn_ref,
     moe_ref,
+    q_ref,
+    new_ref,
+    raw_scale_ref,
+    table_ref,
+    lengths_ref,
+    routes_ref,
+    router_ref,
+    scale_ref,
+    meta_ref,
     x,
     pool,
     scales,
@@ -179,7 +190,10 @@
     acc,
     w_sem,
     own_sem,
-    ag_s,
+    in_sem,
+    ag_zs,
+    ag_ys,
+    ag_cs,
     ag_r,
     kv_s,
     kv_r,
@@ -187,10 +201,12 @@
     sc_r,
     rs_s,
     rs_r,
+    rz_s,
+    rz_r,
 ):
-    rows, width = hid_ref.shape
+    rows, width = hid_hbm.shape
     ff = wg.shape[1]
-    experts = router_ref.shape[1]
+    experts = router_ref.shape[0]
     depth = n // 4
     chips = n // 2
     heads = KEY_VALUE_HEADS
@@ -204,6 +220,24 @@
     def at(zz, yy, cc):
         return zz * 4 + yy * 2 + cc
 
+    own_x = x.at[me, :, pl.ds(0, width)]
+    loads = [
+        pltpu.make_async_copy(src, dst, in_sem.at[i])
+        for i, (src, dst) in enumerate(
+            (
+                (hid_hbm, own_x),
+                (router_hbm, router_ref),
+                (routes_hbm, routes_ref),
+                (table_hbm, table_ref),
+                (lengths_hbm, lengths_ref),
+                (raw_scale_hbm, raw_scale_ref),
+                (q_hbm, q_ref),
+                (new_hbm, new_ref),
+            )
+        )
+    ]
+    for load in loads:
+        load.start()
     weights = [
         pltpu.make_async_copy(s, d, w_sem.at[i])
         for i, (s, d) in enumerate(((wg_hbm, wg), (wu_hbm, wu), (wd_hbm, wd)))
@@ -219,29 +253,36 @@
             barrier, inc=1, device_id={"expert": (me + k) % n}, device_id_type=MESH
         )
 
-    logits = jnp.dot(hid_ref[...], router_ref[...], preferred_element_type=F32)
-    lane = lax.broadcasted_iota(jnp.int32, (rows, experts), 1)
-    chosen = lane < 0
-    for k in range(routes_ref.shape[1]):
-        chosen = jnp.logical_or(chosen, routes_ref[:, k : k + 1] == lane)
+    for load in loads[:3]:
+        load.wait()
+    logits = lax.dot_general(
+        router_ref[...],
+        x[me, :, :width],
+        (((1,), (1,)), ((), ())),
+        preferred_element_type=F32,
+    )
+    expert = lax.broadcasted_iota(jnp.int32, (experts, rows), 0)
+    chosen = expert < 0
+    for k in range(routes_ref.shape[0]):
+        chosen = jnp.logical_or(chosen, routes_ref[k : k + 1, :] == expert)
     logits = jnp.where(chosen, logits, -1e30)
-    terms = jnp.where(chosen, jnp.exp(logits - jnp.max(logits, axis=1, keepdims=True)), 0.0)
-    gates = (terms / jnp.sum(terms, axis=1, keepdims=True)).astype(BF16)
+    terms = jnp.where(chosen, jnp.exp(logits - jnp.max(logits, axis=0, keepdims=True)), 0.0)
+    gates = (terms / jnp.sum(terms, axis=0, keepdims=True)).astype(BF16)
     spread = (
         lax.broadcasted_iota(jnp.int32, (experts, 128), 0)
         == lax.broadcasted_iota(jnp.int32, (experts, 128), 1)
     ).astype(BF16)
-    x[me, :, :width] = hid_ref[...]
-    x[me, :, width:] = jnp.dot(gates, spread, preferred_element_type=F32).astype(BF16)
-    scales[me] = scale_ref[me]
+    x[me, :, width:] = lax.dot_general(
+        gates, spread, (((0,), (0,)), ((), ())), preferred_element_type=F32
+    ).astype(BF16)
 
     pl.semaphore_wait(barrier, n - 1)
 
-    def ag(src, slot, target):
+    def ag(src, send, target):
         return pltpu.make_async_remote_copy(
             src_ref=x.at[src],
             dst_ref=x.at[src],
-            send_sem=ag_s.at[slot],
+            send_sem=send,
             recv_sem=ag_r.at[src],
             device_id={"expert": target},
             device_id_type=MESH,
@@ -267,18 +308,68 @@
             device_id_type=MESH,
         )
 
-    for d in range(1, depth):
-        ag(me, d - 1, at((z + d) % depth, y, c)).start()
-    ag(me, depth - 1, at(z, 1 - y, c)).start()
-    ag(me, 2 * depth - 1, sibling).start()
-
-    kv_order = [sibling]
-    for j in range(1, chips):
-        for cc in range(2):
-            kv_order.append(((chip + j) % chips) * 2 + (c + cc) % 2)
+    last = depth - 1
+
+    def ag_up(zz):
+        return ag(at(zz, y, c), ag_zs.at[0, zz], at(jnp.minimum(z + 1, last), y, c))
+
+    def ag_down(zz):
+        return ag(at(zz, y, c), ag_zs.at[1, zz], at(jnp.maximum(z - 1, 0), y, c))
+
+    def ag_y(zz):
+        return ag(at(zz, y, c), ag_ys.at[zz], at(z, 1 - y, c))
+
+    def ag_core(zz, yy):
+        return ag(at(zz, yy, c), ag_cs.at[zz * 2 + yy], sibling)
+
+    def arrived(src):
+        ag(src, ag_cs.at[0], sibling).wait_recv()
+
+    @pl.when(z < last)
+    def _():
+        ag_up(z).start()
+
+    @pl.when(z > 0)
+    def _():
+        ag_down(z).start()
+
+    ag_y(z).start()
+    ag_core(z, y).start()
+
+    z_far = ((z + depth // 2) % depth, last - z)
+    z_near = (z // 2) * 2 + (1 - z % 2)
+    chip_order = [zz * 2 + yy for zz in z_far for yy in (y, 1 - y)]
+    chip_order += [z_near * 2 + y, z_near * 2 + 1 - y, z * 2 + 1 - y]
+    kv_order = [cc * 2 + k for cc in chip_order for k in (c, 1 - c)] + [sibling]
+
+    for load in loads[3:]:
+        load.wait()
+    kinds, inner, blocks = raw_scale_ref.shape
+    raw = raw_scale_ref[...].reshape(kinds * inner, blocks)
+    per_dest = blocks // n
+    for dest in range(n):
+        pick = (
+            lax.broadcasted_iota(jnp.int32, (blocks, tokens), 0)
+            == dest * per_dest + lax.broadcasted_iota(jnp.int32, (blocks, tokens), 1) // inner
+        ).astype(BF16)
+        wide = jnp.dot(raw, pick, preferred_element_type=F32).reshape(kinds, inner, tokens)
+        keep = lax.broadcasted_iota(jnp.int32, (kinds, inner, tokens), 1) == (
+            lax.broadcasted_iota(jnp.int32, (kinds, inner, tokens), 2) % inner
+        )
+        scale_ref[dest, 0:kinds, :] = jnp.sum(jnp.where(keep, wide, 0.0), axis=1)
+        scale_ref[dest, kinds:, :] = jnp.zeros((8 - kinds, tokens), F32)
     for dest in kv_order:
         sc(dest, me).start()
-        kv(dest, me).start()
+    scales[me] = scale_ref[me]
+    eye = lax.broadcasted_iota(jnp.int32, (rows, rows), 0) == lax.broadcasted_iota(
+        jnp.int32, (rows, rows), 1
+    )
+    length_col = jnp.sum(jnp.where(eye, lengths_ref[...], 0), axis=1, keepdims=True)
+    for b in range(table_ref.shape[0]):
+        rr = slice(b * rows, (b + 1) * rows)
+        col = jnp.sum(jnp.where(eye, table_ref[b : b + 1, :], 0), axis=1, keepdims=True)
+        meta_ref[0, rr, :] = jnp.broadcast_to(col, (rows, 128))
+        meta_ref[1, rr, :] = jnp.broadcast_to(length_col - b * 16, (rows, 128))
 
     req_of_row = lax.broadcasted_iota(jnp.int32, (group * rows, 1), 0) % rows
     for h in range(heads):
@@ -290,24 +381,58 @@
         for g in range(group):
             own = jnp.sum(
                 qh[h, g * rows : (g + 1) * rows, :].astype(F32) * k_new, axis=1, keepdims=True
-            ) * (1.0 / math.sqrt(HEAD_SIZE))
+            ) * LOG2_SCALE
             m_ref[h, g * rows : (g + 1) * rows, :] = jnp.broadcast_to(own, (rows, HEAD_SIZE))
             acc[h, g * rows : (g + 1) * rows, :] = v_new
         first = lax.broadcasted_iota(jnp.int32, (group * rows, HEAD_SIZE), 1) == 0
         l_ref[h] = jnp.where(first, 1.0, 0.0)
 
     for d in range(1, depth):
-        src = at((z + depth - d) % depth, y, c)
-        ag(src, 0, sibling).wait_recv()
-        ag(src, depth - 1 + d, at(z, 1 - y, c)).start()
-        ag(src, 2 * depth - 1 + d, sibling).start()
-    for d in range(depth):
-        src = at((z + depth - d) % depth, 1 - y, c)
-        ag(src, 0, sibling).wait_recv()
-        ag(src, 3 * depth - 1 + d, sibling).start()
+
+        @pl.when(z >= d)
+        def _():
+            zz = jnp.maximum(z - d, 0)
+            arrived(at(zz, y, c))
+
+            @pl.when(z < last)
+            def _():
+                ag_up(zz).start()
+
+            ag_y(zz).start()
+            ag_core(zz, y).start()
+
+        @pl.when(z + d <= last)
+        def _():
+            zz = jnp.minimum(z + d, last)
+            arrived(at(zz, y, c))
+
+            @pl.when(z > 0)
+            def _():
+                ag_down(zz).start()
+
+            ag_y(zz).start()
+            ag_core(zz, y).start()
+
+    def from_y(zz):
+        arrived(at(zz, 1 - y, c))
+        ag_core(zz, 1 - y).start()
+
+    from_y(z)
+    for d in range(1, depth):
+
+        @pl.when(z >= d)
+        def _():
+            from_y(jnp.maximum(z - d, 0))
+
+        @pl.when(z + d <= last)
+        def _():
+            from_y(jnp.minimum(z + d, last))
+
+    for dest in kv_order[0:15]:
+        kv(dest, me).start()
     for zz in range(depth):
         for yy in range(2):
-            ag(at(zz, yy, 1 - c), 0, sibling).wait_recv()
+            arrived(at(zz, yy, 1 - c))
 
     weights[0].wait()
     weights[1].wait()
@@ -352,12 +477,33 @@
     def to_y(zz):
         return rs(part.at[at(zz, 1 - y, c)], r2.at[zz], 2 * depth + zz, at(z, 1 - y, c))
 
-    def to_z(d):
-        there = at((z + d) % depth, y, c)
-        return rs(part.at[there], r3.at[d - 1], 3 * depth + d - 1, there)
+    def rz(way, zt):
+        target = jnp.minimum(z + 1, last) if way == 0 else jnp.maximum(z - 1, 0)
+        return pltpu.make_async_remote_copy(
+            src_ref=part.at[at(zt, y, c)],
+            dst_ref=r3.at[way, zt],
+            send_sem=rz_s.at[way, zt],
+            recv_sem=rz_r.at[way, zt],
+            device_id={"expert": at(target, y, c)},
+            device_id_type=MESH,
+        )
+
+    def step_z(way, zt):
+        ahead = z < zt if way == 0 else z > zt
+        inner_device = z > 0 if way == 0 else z < last
+
+        @pl.when(ahead)
+        def _():
+            @pl.when(inner_device)
+            def _():
+                rz(way, zt).wait_recv()
+                there = at(zt, y, c)
+                part[there] = (part[there].astype(F32) + r3[way, zt].astype(F32)).astype(BF16)
+
+            rz(way, zt).start()
 
     def attend_chip(j):
-        src_chip = (chip + chips - j) % chips
+        src_chip = chip if j == 0 else chip_order[j - 1]
         if j == 0:
             own_kv.wait()
             kv(sibling, sibling).wait_recv()
@@ -369,13 +515,13 @@
                 sc(sibling, src).wait_recv()
         span = 2 * tokens
         peer_blocks = tokens // 16
-        lanes = lax.broadcasted_iota(jnp.int32, (meta_ref.shape[0], span), 1)
-        entry = lax.broadcasted_iota(jnp.int32, (meta_ref.shape[0], span), 0)
+        lanes = lax.broadcasted_iota(jnp.int32, (meta_ref.shape[1], span), 1)
+        entry = lax.broadcasted_iota(jnp.int32, (meta_ref.shape[1], span), 0)
         slot = src_chip * 2 * peer_blocks + lanes // 16
         live = jnp.logical_and(
-            meta_ref[:, 0:1] == slot, (entry % 4) * 16 + lanes % 16 < meta_ref[:, 1:2]
-        )
-        owner = jnp.sum(jnp.where(live, entry // 4 + 1, 0), axis=0, keepdims=True) - 1
+            meta_ref[0, :, 0:1] == slot, lanes % 16 < meta_ref[1, :, 0:1]
+        )
+        owner = jnp.sum(jnp.where(live, entry % rows + 1, 0), axis=0, keepdims=True) - 1
         pair = pl.ds(src_chip * 2, 2)
 
         for h in range(heads):
@@ -385,7 +531,7 @@
             )
             k_scale = jnp.concatenate(
                 [scales[src_chip * 2, h : h + 1, :], scales[src_chip * 2 + 1, h : h + 1, :]], axis=1
-            ) * (1.0 / math.sqrt(HEAD_SIZE))
+            ) * LOG2_SCALE
             v_scale = jnp.concatenate(
                 [
                     scales[src_chip * 2, heads + h : heads + h + 1, :],
@@ -396,7 +542,7 @@
             step = 128
 
             def body(t, _):
-                rr = pl.ds(pl.multiple_of(t * step, step), step)
+                rr = pl.ds(t * step, step)
                 s = lax.dot_general(
                     qh[h, rr, :], keys, (((1,), (1,)), ((), ())), preferred_element_type=F32
                 )
@@ -404,15 +550,15 @@
                 s = jnp.where(req == owner, s * k_scale, -1e30)
                 m_old = m_ref[h, rr, :]
                 m_new = jnp.maximum(m_old, jnp.max(s, axis=1, keepdims=True))
-                p = jnp.exp(s - jnp.concatenate([m_new, m_new], axis=1))
-                alpha = jnp.exp(m_old - m_new)
+                p = jnp.exp2(s - jnp.concatenate([m_new, m_new], axis=1))
+                alpha = jnp.exp2(m_old - m_new)
                 m_ref[h, rr, :] = m_new
                 l_ref[h, rr, :] = alpha * l_ref[h, rr, :] + p[:, :tokens] + p[:, tokens:]
                 mix = jnp.dot((p * v_scale).astype(BF16), vals, preferred_element_type=F32)
                 acc[h, rr, :] = alpha * acc[h, rr, :] + mix
                 return 0
 
-            lax.fori_loop(0, group * rows // step, body, 0)
+            lax.fori_loop(0, group * rows // step, body, 0, unroll=True)
 
     for zz in range(depth):
         to_sibling(zz, 1 - y).start()
@@ -429,20 +575,52 @@
         there = at(zz, y, c)
         part[there] = (part[there].astype(F32) + r1[zz * 2 + y].astype(F32)).astype(BF16)
     attend_chip(1)
-    for d in range(1, depth):
-        zz = (z + d) % depth
+    for zz in range(depth):
         to_y(zz).wait_recv()
         there = at(zz, y, c)
         part[there] = (part[there].astype(F32) + r2[zz].astype(F32)).astype(BF16)
-        to_z(d).start()
-    to_y(z).wait_recv()
+
+        @pl.when(jnp.logical_and(z == 0, zz > 0))
+        def _():
+            if zz > 0:
+                step_z(0, zz)
+
+        @pl.when(jnp.logical_and(z == last, zz < last))
+        def _():
+            if zz < last:
+                step_z(1, zz)
+
+    @pl.when(z > 0)
+    def _():
+        for zt in range(last, 0, -1):
+            step_z(0, zt)
+
+    @pl.when(z < last)
+    def _():
+        for zt in range(last):
+            step_z(1, zt)
+
     for j in range(2, chips):
         attend_chip(j)
-    total = part[me].astype(F32) + r2[z].astype(F32)
-    for d in range(1, depth):
-        to_z(d).wait_recv()
-        total = total + r3[d - 1].astype(F32)
-    moe_ref[...] = total.astype(BF16)
+    @pl.when(z > 0)
+    def _():
+        rz(0, z).wait_recv()
+        r1[0] = r3[0, z]
+
+    @pl.when(z == 0)
+    def _():
+        r1[0] = jnp.zeros((rows, width), BF16)
+
+    @pl.when(z < last)
+    def _():
+        rz(1, z).wait_recv()
+        r1[1] = r3[1, z]
+
+    @pl.when(z == last)
+    def _():
+        r1[1] = jnp.zeros((rows, width), BF16)
+
+    moe_ref[...] = (part[me].astype(F32) + r1[0].astype(F32) + r1[1].astype(F32)).astype(BF16)
 
     for h in range(heads):
         for g in range(group):
@@ -451,8 +629,19 @@
             norm = jnp.sum(l_ref[h, rr, :], axis=1, keepdims=True)
             attn_ref[:, at_lane : at_lane + HEAD_SIZE] = (acc[h, rr, :] / norm).astype(BF16)
 
-    for i in range(n - 1):
-        ag(me, i, sibling).wait_send()
+    for zz in range(depth):
+
+        @pl.when(jnp.logical_and(z < last, zz <= z))
+        def _():
+            ag_up(zz).wait_send()
+
+        @pl.when(jnp.logical_and(z > 0, zz >= z))
+        def _():
+            ag_down(zz).wait_send()
+
+        ag_y(zz).wait_send()
+        for yy in range(2):
+            ag_core(zz, yy).wait_send()
     for dest in kv_order:
         sc(dest, me).wait_send()
         kv(dest, me).wait_send()
@@ -460,8 +649,15 @@
         for yy in range(2):
             to_sibling(zz, yy).wait_send()
         to_y(zz).wait_send()
-    for d in range(1, depth):
-        to_z(d).wait_send()
+    for zt in range(depth):
+
+        @pl.when(z < zt)
+        def _():
+            rz(0, zt).wait_send()
+
+        @pl.when(z > zt)
+        def _():
+            rz(1, zt).wait_send()
 
 
 def fused_local(
@@ -486,17 +682,10 @@
     depth = n // 4
     codes = key_value_codes.reshape(n, tokens, features)
     kinds = key_value_scales.shape[1]
-    scales = jnp.transpose(
-        key_value_scales.reshape(n, blocks // n, kinds, block_tokens), (0, 2, 1, 3)
-    ).reshape(n, kinds, tokens)
-    scales = jnp.pad(scales.astype(jnp.float32), ((0, 0), (0, 8 - kinds), (0, 0)))
-    table = block_table[0]
-    meta = jnp.stack(
-        [table.reshape(-1), jnp.broadcast_to(lengths[0][:, None], table.shape).reshape(-1)], axis=1
-    )
+    per_request = block_table.shape[2]
     q_rows = rows * QUERY_HEADS // KEY_VALUE_HEADS
     vmem = pl.BlockSpec(memory_space=pltpu.VMEM)
-    hbm = pl.BlockSpec(memory_space=pl.ANY)
+    hbm = pl.BlockSpec(memory_space=pltpu.HBM)
     dma = pltpu.SemaphoreType.DMA
     return pl.pallas_call(
         functools.partial(fused_kernel, n),
@@ -504,9 +693,18 @@
             jax.ShapeDtypeStruct(queries.shape, BF16),
             jax.ShapeDtypeStruct(hidden.shape, BF16),
         ),
-        in_specs=[vmem, vmem, hbm, vmem, vmem, vmem, vmem, vmem, hbm, hbm, hbm],
+        in_specs=[hbm] * 12,
         out_specs=(vmem, vmem),
         scratch_shapes=[
+            pltpu.VMEM(queries.shape, BF16),
+            pltpu.VMEM(incoming_key_value.shape, BF16),
+            pltpu.VMEM((kinds, block_tokens, blocks), BF16),
+            pltpu.VMEM((per_request, rows), jnp.int32),
+            pltpu.VMEM((1, rows), jnp.int32),
+            pltpu.VMEM((routes.shape[1], rows), jnp.int32),
+            pltpu.VMEM((router.shape[1], width), BF16),
+            pltpu.VMEM((n, 8, tokens), F32),
+            pltpu.VMEM((2, per_request * rows, 128), jnp.int32),
             pltpu.VMEM((n, rows, width + 128), BF16),
             pltpu.VMEM((n, tokens, features), BF16),
             pltpu.VMEM((n, 8, tokens), F32),
@@ -517,34 +715,40 @@
             pltpu.VMEM((n, rows, width), BF16),
             pltpu.VMEM((2 * depth, rows, width), BF16),
             pltpu.VMEM((depth, rows, width), BF16),
-            pltpu.VMEM((depth - 1, rows, width), BF16),
+            pltpu.VMEM((2, depth, rows, width), BF16),
             pltpu.VMEM((KEY_VALUE_HEADS, q_rows, HEAD_SIZE), BF16),
             pltpu.VMEM((KEY_VALUE_HEADS, q_rows, HEAD_SIZE), F32),
             pltpu.VMEM((KEY_VALUE_HEADS, q_rows, HEAD_SIZE), F32),
             pltpu.VMEM((KEY_VALUE_HEADS, q_rows, HEAD_SIZE), F32),
             dma((3,)),
             dma((1,)),
-            dma((n - 1,)),
+            dma((8,)),
+            dma((2, depth)),
+            dma((depth,)),
+            dma((2 * depth,)),
             dma((n,)),
             dma((n,)),
             dma((n,)),
             dma((n,)),
             dma((n,)),
-            dma((n - 1,)),
-            dma((n - 1,)),
+            dma((3 * depth,)),
+            dma((3 * depth,)),
+            dma((2, depth)),
+            dma((2, depth)),
         ],
         compiler_params=pltpu.CompilerParams(
-            collective_id=0, has_side_effects=True, vmem_limit_bytes=48 * 1024 * 1024
+            collective_id=0, has_side_effects=True, vmem_limit_bytes=63 * 1024 * 1024
         ),
     )(
         queries,
         incoming_key_value,
         codes,
-        scales,
-        meta,
+        jnp.transpose(key_value_scales, (1, 2, 0)),
+        jnp.transpose(block_table[0]),
+        lengths,
         hidden,
-        routes,
-        router,
+        jnp.transpose(routes),
+        jnp.transpose(router),
         w_gate[0],
         w_up[0],
         w_down[0],

time: 107 us -> 85.6 us (0.80)
  the two profiles are of different devices: /device:TPU:9 before, /device:TPU:0 now
where the time goes in v2:
time: 85.6 us; the launch traced here: 85.4 us
  Pallas kernels  81.5 us (95%)
  local copies, waits for them, and re-layouts  3.24 us (4%)
    pallas_call x1, Pallas kernels, fused_local(): pl.pallas_call(functools.partial(fused_kernel, n), out_shape=(jax.ShapeDt...  81.5 us
    unnamed x2, local copies, waits for them, and re-layouts  3.24 us

profile of v2, /device:TPU:0, one launch (start us, length us, event | category | flops | bytes accessed | tf_op | source)
XLA Modules:
  0.0 85.4 jit_solution(3564296643368932724)
XLA Ops:
  0.6 81.5 %shard_map.131 = (bf16[32,4096]{1,0:T(8,128)(2,1)}, bf16[32,2048]{1,0:T(8,128)(2,1)}) custom-call(bf16[32,4096]{1,0:T(8,128)(2,1)} %q_hbm.1, bf16[32,512]{1,0:T(8,128)(2,1)} %new_hbm.1, bf16[16,128,512]{2,1,0:T(8,128)(2,1)} %bitcast.13, bf16[4,16,128]{2,1,0:T(8,128)(2,1)} %bitcast.15, s32[4,32]{1,0:T(4,128)} %bitcast.17, s32[1,32]{1,0:T(1,128)} %lengths_hbm.1, ...), custom_call_target="tpu_custom_call" | custom-call | tf_op jit(solution)/shard_map/pallas_call | solution.py:690
  82.2 1.7 %copy.16 = bf16[32,4096]{1,0:T(8,128)(2,1)} copy(bf16[32,4096]{1,0:T(8,128)(2,1)} %get-tuple-element.4) | data formatting | bytes 524288
  83.8 1.6 %copy.17 = bf16[32,2048]{1,0:T(8,128)(2,1)} copy(bf16[32,2048]{1,0:T(8,128)(2,1)} %get-tuple-element.5) | data formatting | bytes 262144

commit v3 on v2

--- a/solution.py
+++ b/solution.py
@@ -201,8 +201,6 @@
     sc_r,
     rs_s,
     rs_r,
-    rz_s,
-    rz_r,
 ):
     rows, width = hid_hbm.shape
     ff = wg.shape[1]
@@ -477,30 +475,9 @@
     def to_y(zz):
         return rs(part.at[at(zz, 1 - y, c)], r2.at[zz], 2 * depth + zz, at(z, 1 - y, c))
 
-    def rz(way, zt):
-        target = jnp.minimum(z + 1, last) if way == 0 else jnp.maximum(z - 1, 0)
-        return pltpu.make_async_remote_copy(
-            src_ref=part.at[at(zt, y, c)],
-            dst_ref=r3.at[way, zt],
-            send_sem=rz_s.at[way, zt],
-            recv_sem=rz_r.at[way, zt],
-            device_id={"expert": at(target, y, c)},
-            device_id_type=MESH,
-        )
-
-    def step_z(way, zt):
-        ahead = z < zt if way == 0 else z > zt
-        inner_device = z > 0 if way == 0 else z < last
-
-        @pl.when(ahead)
-        def _():
-            @pl.when(inner_device)
-            def _():
-                rz(way, zt).wait_recv()
-                there = at(zt, y, c)
-                part[there] = (part[there].astype(F32) + r3[way, zt].astype(F32)).astype(BF16)
-
-            rz(way, zt).start()
+    def to_z(d):
+        there = at((z + d) % depth, y, c)
+        return rs(part.at[there], r3.at[d - 1], 3 * depth + d - 1, there)
 
     def attend_chip(j):
         src_chip = chip if j == 0 else chip_order[j - 1]
@@ -575,52 +552,20 @@
         there = at(zz, y, c)
         part[there] = (part[there].astype(F32) + r1[zz * 2 + y].astype(F32)).astype(BF16)
     attend_chip(1)
-    for zz in range(depth):
+    for d in range(1, depth + 1):
+        zz = (z + d) % depth
         to_y(zz).wait_recv()
         there = at(zz, y, c)
         part[there] = (part[there].astype(F32) + r2[zz].astype(F32)).astype(BF16)
-
-        @pl.when(jnp.logical_and(z == 0, zz > 0))
-        def _():
-            if zz > 0:
-                step_z(0, zz)
-
-        @pl.when(jnp.logical_and(z == last, zz < last))
-        def _():
-            if zz < last:
-                step_z(1, zz)
-
-    @pl.when(z > 0)
-    def _():
-        for zt in range(last, 0, -1):
-            step_z(0, zt)
-
-    @pl.when(z < last)
-    def _():
-        for zt in range(last):
-            step_z(1, zt)
-
+        if d < depth:
+            to_z(d).start()
     for j in range(2, chips):
         attend_chip(j)
-    @pl.when(z > 0)
-    def _():
-        rz(0, z).wait_recv()
-        r1[0] = r3[0, z]
-
-    @pl.when(z == 0)
-    def _():
-        r1[0] = jnp.zeros((rows, width), BF16)
-
-    @pl.when(z < last)
-    def _():
-        rz(1, z).wait_recv()
-        r1[1] = r3[1, z]
-
-    @pl.when(z == last)
-    def _():
-        r1[1] = jnp.zeros((rows, width), BF16)
-
-    moe_ref[...] = (part[me].astype(F32) + r1[0].astype(F32) + r1[1].astype(F32)).astype(BF16)
+    total = part[me].astype(F32)
+    for d in range(1, depth):
+        to_z(d).wait_recv()
+        total = total + r3[d - 1].astype(F32)
+    moe_ref[...] = total.astype(BF16)
 
     for h in range(heads):
         for g in range(group):
@@ -649,15 +594,8 @@
         for yy in range(2):
             to_sibling(zz, yy).wait_send()
         to_y(zz).wait_send()
-    for zt in range(depth):
-
-        @pl.when(z < zt)
-        def _():
-            rz(0, zt).wait_send()
-
-        @pl.when(z > zt)
-        def _():
-            rz(1, zt).wait_send()
+    for d in range(1, depth):
+        to_z(d).wait_send()
 
 
 def fused_local(
@@ -715,7 +653,7 @@
             pltpu.VMEM((n, rows, width), BF16),
             pltpu.VMEM((2 * depth, rows, width), BF16),
             pltpu.VMEM((depth, rows, width), BF16),
-            pltpu.VMEM((2, depth, rows, width), BF16),
+            pltpu.VMEM((depth - 1, rows, width), BF16),
             pltpu.VMEM((KEY_VALUE_HEADS, q_rows, HEAD_SIZE), BF16),
             pltpu.VMEM((KEY_VALUE_HEADS, q_rows, HEAD_SIZE), F32),
             pltpu.VMEM((KEY_VALUE_HEADS, q_rows, HEAD_SIZE), F32),
@@ -731,10 +669,8 @@
             dma((n,)),
             dma((n,)),
             dma((n,)),
-            dma((3 * depth,)),
-            dma((3 * depth,)),
-            dma((2, depth)),
-            dma((2, depth)),
+            dma((n - 1,)),
+            dma((n - 1,)),
         ],
         compiler_params=pltpu.CompilerParams(
             collective_id=0, has_side_effects=True, vmem_limit_bytes=63 * 1024 * 1024

time: 85.6 us -> 83.2 us (0.972)
  the two profiles are of different devices: /device:TPU:0 before, /device:TPU:9 now
where the time goes in v3:
time: 83.2 us; the launch traced here: 81.6 us
  Pallas kernels  77.7 us (93%)
  local copies, waits for them, and re-layouts  3.24 us (4%)
    pallas_call x1, Pallas kernels, fused_local(): pl.pallas_call(functools.partial(fused_kernel, n), out_shape=(jax.ShapeDt...  77.7 us
    unnamed x2, local copies, waits for them, and re-layouts  3.24 us

profile of v3, /device:TPU:9, one launch (start us, length us, event | category | flops | bytes accessed | tf_op | source)
XLA Modules:
  0.0 81.6 jit_solution(3960983577928227461)
XLA Ops:
  0.6 77.7 %shard_map.131 = (bf16[32,4096]{1,0:T(8,128)(2,1)}, bf16[32,2048]{1,0:T(8,128)(2,1)}) custom-call(bf16[32,4096]{1,0:T(8,128)(2,1)} %q_hbm.1, bf16[32,512]{1,0:T(8,128)(2,1)} %new_hbm.1, bf16[16,128,512]{2,1,0:T(8,128)(2,1)} %bitcast.13, bf16[4,16,128]{2,1,0:T(8,128)(2,1)} %bitcast.15, s32[4,32]{1,0:T(4,128)} %bitcast.17, s32[1,32]{1,0:T(1,128)} %lengths_hbm.1, ...), custom_call_target="tpu_custom_call" | custom-call | tf_op jit(solution)/shard_map/pallas_call | solution.py:628
  78.3 1.7 %copy.16 = bf16[32,4096]{1,0:T(8,128)(2,1)} copy(bf16[32,4096]{1,0:T(8,128)(2,1)} %get-tuple-element.4) | data formatting | bytes 524288
  80.0 1.6 %copy.17 = bf16[32,2048]{1,0:T(8,128)(2,1)} copy(bf16[32,2048]{1,0:T(8,128)(2,1)} %get-tuple-element.5) | data formatting | bytes 262144
